TPU v7x, 256 devices: a whole 4x4x8 slice. The times are simulated.
256 devices in a mesh: row: 32 (over y, x, core), col: 8 (over z).
Axes of the slice: x: 4, y: 4, z: 8, core: 2. Of those that a mesh axis runs over, the one named last changes fastest.
Arguments:
- factor: float32 [2, 4096, 20, 4096], P(None, 'row', None, 'col'), as said below
- inverses: float32 [2, 4096, 4096], P(None, 'col', 'row'), as said below
- right_side: float32 [2, 4096, 64], P(None, 'row'), may hold values from -6 to 6
- earlier: float32 [18, 4096, 64], P(None, ('col', 'row')), may hold values from -6 to 6
Outputs:
- solved: float32 [2, 4096, 64], P(None, 'col')
Inputs may be any that keep to these rules, and one draw needn't show every extreme that they name: factor[k] is zero in every block of centres numbered 18 + k or higher. Each inverses[k] is lower triangular with a positive diagonal.
All inputs are finite; a program needn't handle non-finite values.
Results may differ from a plain program's by a relative error of at most 0.0001.
Values sent between devices are 32-bit elements; how exact they have to be, the bound alone decides.
A program may use at most 128 MiB of HBM per device.

v0:
```python
import jax
import jax.numpy as jnp
from jax import lax
from jax.sharding import PartitionSpec as P


def contract(tiles, values):
    return jnp.einsum(
        "srkc,kcq->srq",
        tiles,
        values,
        precision=lax.Precision.HIGHEST,
        preferred_element_type=jnp.float32,
    )


def column_total(partial_value):
    return lax.psum(partial_value, "col")


def local(factor, inverses, right_side, earlier):
    steps = factor.shape[0]
    prior = earlier.shape[0]
    highest = lax.Precision.HIGHEST
    leading = factor[:, :, :prior, :]
    results = []
    partial_value = contract(leading, lax.all_gather(earlier, "row", axis=1, tiled=True))
    for step in range(steps):
        total = column_total(partial_value[step])
        residue = right_side[step] - total
        term = jnp.dot(
            inverses[step], residue, precision=highest, preferred_element_type=jnp.float32
        )
        value = lax.psum(term, "row")
        results.append(value)
        if step + 1 < steps:
            update = jnp.einsum(
                "src,cq->srq",
                factor[step + 1 :, :, prior + step, :],
                value,
                precision=highest,
                preferred_element_type=jnp.float32,
            )
            partial_value = partial_value.at[step + 1 :].add(update)
    return jnp.stack(results)


def solution(mesh):
    in_specs = (
        P(None, "row", None, "col"),
        P(None, "col", "row"),
        P(None, "row", None),
        P(None, ("col", "row"), None),
    )
    out_specs = P(None, "col", None)
    return jax.shard_map(local, mesh=mesh, in_specs=in_specs, out_specs=out_specs, check_vma=False)
```

profile of v0, /device:TPU:1, one launch (start us, length us, event | category | flops | bytes accessed | tf_op | source)
XLA Modules:
  0.0 366.2 jit_solution(6058327458823033554)
XLA Ops:
  6.5 0.0 copy-start.1
  6.5 0.0 copy-start
  6.5 0.0 all-gather.2.cloned.1.call-start
  6.5 0.7 all-gather.2.cloned.1.call-update
  7.3 0.0 all-reduce.3.cloned.1.call-start
  7.3 62.3 %all-gather.2.cloned.1.call-done = f32[18,512,64]{2,1,0:T(8,128)} async-done(((f32[18,16,64]{2,1,0:T(8,128)}), f32[18,512,64]{2,1,0:T(8,128)}) %all-gather.2.cloned.1.call-update) | async-done | bytes 2359312 | tf_op jit(solution)/shard_map/all_gather | solution.py:27
  69.6 11.0 %fusion.2 = f32[2,128,64]{1,2,0:T(8,128)S(1)} fusion(f32[2,128,20,512]{3,1,2,0:T(8,128)} %param.6, f32[18,512,64]{2,1,0:T(8,128)} %all-gather.2.cloned.1.call-done), kind=kOutput, calls=%fused_computation.4 | convolution fusion | flops 1811939328 | bytes 12910592 | tf_op jit(solution)/shard_map/srkc,kcq->srq/dot_general | solution.py:8
  80.7 23.1 %psum.28 = f32[128,64]{0,1:T(8,128)S(1)} all-reduce(f32[128,64]{0,1:T(8,128)S(1)} %slice_bitcast_fusion), channel_id=1, replica_groups=mesh['row'=32,'col'=8] {'col'}, use_global_device_ids=true, to_apply=%region_0.0 | all-reduce | flops 8192 | bytes 65536 | tf_op jit(solution)/shard_map/psum | solution.py:18
  103.8 0.0 copy-done.1
  103.8 0.0 copy-done
  103.8 1.0 convolution_bitcast_fusion.1
  104.9 0.0 all-reduce.3.cloned.1.call-update
  104.9 0.0 all-reduce.5.cloned.1.call-start
  104.9 113.6 %all-reduce.3.cloned.1.call-done = f32[512,64]{0,1:T(8,128)} async-done(((f32[512,64]{0,1:T(8,128)}), f32[512,64]{0,1:T(8,128)}) %all-reduce.3.cloned.1.call-update) | async-done | bytes 131088 | tf_op jit(solution)/shard_map/psum | solution.py:34
  218.5 1.4 fusion.6
  219.9 23.0 %psum.30 = f32[128,64]{0,1:T(8,128)S(1)} all-reduce(f32[128,64]{0,1:T(8,128)S(1)} %fusion.6), channel_id=1, replica_groups=mesh['row'=32,'col'=8] {'col'}, use_global_device_ids=true, to_apply=%region_2.0 | all-reduce | flops 8192 | bytes 65536 | tf_op jit(solution)/shard_map/psum | solution.py:18
  242.9 1.0 convolution_bitcast_fusion
  244.0 0.0 all-reduce.5.cloned.1.call-update
  244.0 113.9 %all-reduce.5.cloned.1.call-done = f32[1,512,64]{1,2,0:T(8,128)} async-done(((f32[1,512,64]{1,2,0:T(8,128)}), f32[1,512,64]{1,2,0:T(8,128)}) %all-reduce.5.cloned.1.call-update) | async-done | bytes 131088 | tf_op jit(solution)/shard_map/psum | solution.py:34
  357.9 1.7 pad_maximum_fusion
  (1 shorter events, 0.0 us)
Async XLA Ops:
  6.5 97.3 %copy-start.1 = (f32[2,128,64]{1,2,0:T(8,128)S(1)}, f32[2,128,64]{1,2,0:T(8,128)}, u32[]{:S(2)}) copy-start(f32[2,128,64]{1,2,0:T(8,128)} %param.8) | copy-start | bytes 196612
  6.5 97.3 %copy-start = (f32[2,512,128]{2,1,0:T(8,128)S(1)}, f32[2,512,128]{2,1,0:T(8,128)}, u32[]{:S(2)}) copy-start(f32[2,512,128]{2,1,0:T(8,128)} %param.7) | copy-start | bytes 1572868
  6.5 63.0 %all-gather.2.cloned.1.call-start = ((), (), s32[]{:S(2)}) async-start(), calls=%async_computation | async-start | bytes 4866048 | tf_op jit(solution)/shard_map/all_gather | solution.py:27
  7.3 211.3 %all-reduce.3.cloned.1.call-start = ((), (), s32[]{:S(2)}) async-start(), calls=%async_computation.1 | async-start | bytes 262144 | tf_op jit(solution)/shard_map/psum | solution.py:34
  104.9 253.1 %all-reduce.5.cloned.1.call-start = ((), (), s32[]{:S(2)}) async-start(), calls=%async_computation.2 | async-start | bytes 262144 | tf_op jit(solution)/shard_map/psum | solution.py:34
Sparse Core Ops, SparseCore 0:
  9.8 59.7 all-gather.1
  105.0 113.4 all-reduce.2
  244.1 113.7 all-reduce.4
where the time goes:
time: 366 us
  waiting for transfers between devices  291 us (80%)
  blocking collectives  46.1 us (13%)
  matrix products  14.6 us (4%)
  between operations  13.1 us (4%)
    psum x2, waiting for transfers between devices, local(): value = lax.psum(term, 'row')  228 us
    all_gather x1, waiting for transfers between devices, local(): lax.all_gather(earlier, 'row', axis=1, tiled=True)  62.3 us
    psum x2, blocking collectives, column_total(): return lax.psum(partial_value, 'col')  46.1 us
    dot_general x1, matrix products, contract(): jnp.einsum('srkc,kcq->srq', tiles, values, precision=lax.Precision.HIGHES...  11 us
  transfers between devices with their start and end apart: 3, of which 3 were waited for; matrix products, arithmetic and copies ran while one was open for 0% of the time, Pallas kernels for 0%

commit v1 on v0

v1 whole, which is shorter than its diff:
```python
import functools

import jax
import jax.numpy as jnp
from jax import lax
from jax.experimental import pallas as pl
from jax.experimental.pallas import tpu as pltpu
from jax.sharding import PartitionSpec as P

MESH = pl.DeviceIdType.MESH
F32 = jnp.float32
BF16 = jnp.bfloat16
CORES = 2


def split(value):
    high = value.astype(BF16)
    return high, (value - high.astype(F32)).astype(BF16)


def product(left, right):
    return jnp.dot(left, right, preferred_element_type=F32)


def kernel(
    side, planes, factor, inverses, right_side, earlier, solved,
    known, tiles, tiles_split, corner, inverse, inverse_split, corner_split, sums,
    mine, others, term, parts, pair, value,
    load_sem, send_sem, ring_sem, group_sem, core_sem, z_sem, scatter_sem, pair_sem, gather_sem,
):
    steps, prior, rows, width = tiles.shape
    half = prior // 2
    outs = right_side.shape[1]
    place = lax.axis_index("row")
    z = lax.axis_index("col")
    y, x, core = place // (side * CORES), (place // CORES) % side, place % CORES
    chips = side * side

    def chip_at(dy, dx):
        return (y + dy) % side, (x + dx) % side

    def device(dy, dx):
        to_y, to_x = chip_at(dy, dx)
        return ((to_y * side + to_x) * CORES + core, z)

    def above(dz):
        return (place, (z + dz) % planes)

    sibling = (place + 1 - 2 * core, z)
    around = [(dy, dx) for dy in range(side) for dx in range(side) if (dy, dx) != (0, 0)]

    group = half // 3
    loads = []
    for at in range(prior // group):
        for step in range(steps):
            blocks = pl.ds(at * group, group)
            loads.append(
                pltpu.make_async_copy(
                    factor.at[step, blocks], tiles.at[step, blocks], load_sem.at[len(loads)]
                )
            )
    extra = [
        pltpu.make_async_copy(factor.at[1, prior], corner, load_sem.at[len(loads)]),
        pltpu.make_async_copy(inverses, inverse, load_sem.at[len(loads) + 1]),
    ]
    for copy in loads + extra:
        copy.start()

    barrier = pltpu.get_barrier_semaphore()
    for dy, dx in around:
        pl.semaphore_signal(barrier, inc=1, device_id=device(dy, dx), device_id_type=MESH)
    for dz in range(1, planes):
        pl.semaphore_signal(barrier, inc=1, device_id=above(dz), device_id_type=MESH)
    pl.semaphore_signal(barrier, inc=1, device_id=sibling, device_id_type=MESH)

    outer, inner = (y, x), (x, y)
    for part in range(2):
        for block in range(half):
            rows_of = earlier[part * half + block]
            known[part, core, outer[part], inner[part], block] = jnp.concatenate(
                [rows_of[0:8], rows_of[8:16]], axis=1
            )

    pl.semaphore_wait(barrier, len(around) + planes)

    def ring(part, distance):
        return device(0, distance) if part == 0 else device(distance, 0)

    def across(part, distance):
        return device(distance, 0) if part == 0 else device(0, distance)

    def remote(source, target, send, recv, to):
        return pltpu.make_async_remote_copy(
            src_ref=source, dst_ref=target, send_sem=send, recv_sem=recv, device_id=to, device_id_type=MESH
        )

    def piece(part, distance):
        return known.at[part, core, outer[part], (inner[part] + distance) % side]

    def whole(part, distance):
        return known.at[part, core, (outer[part] + distance) % side]

    order = [d for d in (2, 1, 3) if d < side]
    for distance in order:
        for part in range(2):
            own = piece(part, 0)
            remote(own, own, send_sem.at[0], ring_sem.at[part, distance], ring(part, distance)).start()

    def forward(part, held):
        own = piece(part, held)
        for distance in order:
            remote(own, own, send_sem.at[1], group_sem.at[part, distance], across(part, distance)).start()

    for part in range(2):
        forward(part, 0)

    def cut(at):
        for step in range(steps):
            loads[at * steps + step].wait()

        def one(block, carry):
            for step in range(steps):
                high, low = split(tiles[step, block])
                tiles_split[block, pl.ds(2 * step * rows, rows)] = high
                tiles_split[block, pl.ds((2 * step + 1) * rows, rows)] = low
            return carry

        lax.fori_loop(at * group, (at + 1) * group, one, 0)

    cut(0)
    cut(1)
    for distance in [d for d in (1, 3, 2) if d < side]:
        for part in range(2):
            at = side - distance
            own = piece(part, at)
            remote(own, own, send_sem.at[0], ring_sem.at[part, distance], ring(part, distance)).wait_recv()
            forward(part, at)
    for part in range(2):
        own = whole(part, 0)
        remote(own, own, send_sem.at[2], core_sem.at[part, 0], sibling).start()
    for at in range(2, prior // group):
        cut(at)

    for copy in extra:
        copy.wait()
    for step in range(steps):
        high, low = split(jnp.transpose(inverse[step]))
        inverse_split[step, 0, 0:rows] = high
        inverse_split[step, 0, rows : 2 * rows] = high
        inverse_split[step, 1, 0:rows] = low
        inverse_split[step, 1, rows : 2 * rows] = low
    high, low = split(jnp.transpose(corner[...]))
    corner_split[:, 0:rows] = high
    corner_split[:, rows : 2 * rows] = low

    for distance in [d for d in (1, 3, 2) if d < side]:
        for part in range(2):
            own = whole(part, side - distance)
            remote(own, own, send_sem.at[1], group_sem.at[part, distance], across(part, distance)).wait_recv()
            remote(own, own, send_sem.at[2], core_sem.at[part, distance], sibling).start()
    for distance in range(side):
        for part in range(2):
            own = whole(part, distance)
            remote(own, own, send_sem.at[2], core_sem.at[part, distance], sibling).wait_recv()

    left = lax.broadcasted_iota(jnp.int32, (8, 2 * outs), 1) < outs

    def unpack(packed):
        high = packed.astype(BF16).astype(F32)
        low = packed - high
        first = jnp.where(left, high, pltpu.roll(low, outs, 1))
        second = jnp.where(left, pltpu.roll(high, outs, 1), low)
        return [first, second]

    sums[...] = jnp.zeros_like(sums)
    for part in range(2):

        def block_sum(block, carry, part=part):
            lines = []
            for at_y in range(side):
                for at_x in range(side):
                    for at_core in range(CORES):
                        at = (at_y, at_x) if part == 0 else (at_x, at_y)
                        lines += unpack(known[part, at_core, at[0], at[1], block])
            weights = jnp.concatenate(lines, axis=0).astype(BF16)
            sums[...] += product(tiles_split[part * half + block], weights)
            return carry

        lax.fori_loop(0, half, block_sum, 0)

    def folded(step):
        both = sums[2 * step * rows : (2 * step + 1) * rows] + sums[(2 * step + 1) * rows : (2 * step + 2) * rows]
        turned = jnp.transpose(both)
        return turned[0:outs] + turned[outs : 2 * outs]

    lanes = parts.shape[-1]
    across_lanes = width // lanes

    for step in range(steps):
        partial = folded(step)
        if step > 0:
            last = jnp.concatenate(
                [
                    jnp.concatenate(
                        [value[step - 1, q * across_lanes + l] for l in range(across_lanes)], axis=1
                    )
                    for q in range(chips // across_lanes)
                ],
                axis=0,
            )
            solved[step - 1] = last
            high, low = split(last)
            update = product(jnp.concatenate([high, low], axis=0), corner_split[...])
            update = update[:, 0:rows] + update[:, rows : 2 * rows]
            partial = partial + (update[0:outs] + update[outs : 2 * outs])
        mine[step] = partial
        for dz in [d for d in (4, 3, 5, 2, 6, 1, 7) if d < planes]:
            remote(mine.at[step], others.at[step, dz - 1], send_sem.at[3 + step], z_sem.at[step], above(dz)).start()
        got = others.at[step]
        remote(got, got, send_sem.at[3 + step], z_sem.at[step], sibling).wait_recv()
        total = partial
        for dz in range(planes - 1):
            total = total + others[step, dz]
        high, low = split(right_side[step] - total)
        both = jnp.concatenate([high, low], axis=1)
        result = product(both, inverse_split[step, 0]) + product(both, inverse_split[step, 1])
        for q in range(chips // across_lanes):
            for l in range(across_lanes):
                term[step, q * across_lanes + l] = result[8 * q : 8 * q + 8, l * lanes : (l + 1) * lanes]
        for at, (dy, dx) in enumerate(around):
            to_y, to_x = chip_at(dy, dx)
            remote(
                term.at[step, to_y * side + to_x], parts.at[step, at], send_sem.at[5 + step], scatter_sem.at[step], device(dy, dx)
            ).start()
        got = parts.at[step]
        remote(got, got, send_sem.at[5 + step], scatter_sem.at[step], sibling).wait_recv()
        here = y * side + x
        total = term[step, here]
        for at in range(chips - 1):
            total = total + parts[step, at]
        pair[step, 0] = total
        swap = remote(pair.at[step, 0], pair.at[step, 1], send_sem.at[7 + step], pair_sem.at[step], sibling)
        swap.start()
        swap.wait_recv()
        value[step, here] = total + pair[step, 1]
        for dy, dx in around:
            remote(value.at[step, here], value.at[step, here], send_sem.at[9 + step], gather_sem.at[step], device(dy, dx)).start()
        got = value.at[step, pl.ds(0, chips - 1)]
        remote(got, got, send_sem.at[9 + step], gather_sem.at[step], sibling).wait_recv()

    step = steps - 1
    for q in range(chips // across_lanes):
        for l in range(across_lanes):
            solved[step, 8 * q : 8 * q + 8, l * lanes : (l + 1) * lanes] = value[step, q * across_lanes + l]

    for part in range(2):
        got = known.at[part, 0, 0, pl.ds(0, side - 1)]
        remote(got, got, send_sem.at[0], ring_sem.at[part, 1], sibling).wait_send()
        got = known.at[part, 0, pl.ds(0, side - 1)]
        remote(got, got, send_sem.at[1], ring_sem.at[part, 1], sibling).wait_send()
        got = known.at[part, 0]
        remote(got, got, send_sem.at[2], ring_sem.at[part, 1], sibling).wait_send()
    for step in range(steps):
        for at, got in (
            (3, others.at[step]),
            (5, parts.at[step]),
            (7, pair.at[step, 0]),
            (9, value.at[step, pl.ds(0, chips - 1)]),
        ):
            remote(got, got, send_sem.at[at + step], z_sem.at[step], sibling).wait_send()


def local(side, planes, factor, inverses, right_side, earlier):
    steps, rows, _, width = factor.shape
    prior, share, outs = earlier.shape
    half = prior // 2
    chips = side * side
    lanes = width * outs // (chips * 8)
    dma, vmem = pltpu.SemaphoreType.DMA, pltpu.VMEM
    any_space = pl.BlockSpec(memory_space=pl.ANY)
    in_vmem = pl.BlockSpec(memory_space=pltpu.VMEM)
    solved = pl.pallas_call(
        functools.partial(kernel, side, planes),
        name="falkon",
        out_shape=jax.ShapeDtypeStruct((steps, outs, width), F32),
        in_specs=[any_space, any_space, in_vmem, in_vmem],
        out_specs=in_vmem,
        scratch_shapes=[
            vmem((2, CORES, side, side, half, 8, 2 * outs), F32),
            vmem((steps, prior, rows, width), F32),
            vmem((prior, 2 * steps * rows, width), BF16),
            vmem((rows, width), F32),
            vmem((steps, width, rows), F32),
            vmem((steps, 2, 2 * rows, width), BF16),
            vmem((width, 2 * rows), BF16),
            vmem((2 * steps * rows, 2 * outs), F32),
            vmem((steps, outs, rows), F32),
            vmem((steps, planes - 1, outs, rows), F32),
            vmem((steps, chips, 8, lanes), F32),
            vmem((steps, chips - 1, 8, lanes), F32),
            vmem((steps, 2, 8, lanes), F32),
            vmem((steps, chips, 8, lanes), F32),
            dma((6 * steps + 2,)),
            dma((11,)),
            dma((2, side)),
            dma((2, side)),
            dma((2, side)),
            dma((steps,)),
            dma((steps,)),
            dma((steps,)),
            dma((steps,)),
        ],
        compiler_params=pltpu.CompilerParams(
            collective_id=0, has_side_effects=True, vmem_limit_bytes=48 << 20
        ),
    )(
        jnp.transpose(factor, (0, 2, 1, 3)),
        inverses,
        jnp.transpose(right_side, (0, 2, 1)),
        earlier,
    )
    return jnp.transpose(solved, (0, 2, 1))


def solution(mesh):
    side = 1
    while side * side * CORES < mesh.shape["row"]:
        side += 1
    in_specs = (
        P(None, "row", None, "col"),
        P(None, "col", "row"),
        P(None, "row", None),
        P(None, ("col", "row"), None),
    )
    return jax.shard_map(
        functools.partial(local, side, mesh.shape["col"]),
        mesh=mesh,
        in_specs=in_specs,
        out_specs=P(None, "col", None),
        check_vma=False,
    )
```

time: 366 us -> 70.2 us (0.19)
  waiting for transfers between devices: 291 us -> 0 us
  Pallas kernels: 0 us -> 66.5 us
  blocking collectives: 46.1 us -> 0 us
  matrix products: 14.6 us -> 0 us
  between operations: 13.1 us -> 0.01 us
    psum x2 -> x0, waiting for transfers between devices: 228 us -> none  [local(): value = lax.psum(term, 'row')]
    pallas_call x0 -> x1, Pallas kernels: none -> 66.5 us  [local(): pl.pallas_call(functools.partial(kernel, side, planes), name='falkon', ou...]
    all_gather x1 -> x0, waiting for transfers between devices: 62.3 us -> none  [local(): lax.all_gather(earlier, 'row', axis=1, tiled=True)]
    psum x2 -> x0, blocking collectives: 46.1 us -> none  [column_total(): return lax.psum(partial_value, 'col')]
    dot_general x4 -> x0, matrix products: 14.6 us -> none  [the longest x1 11 us: contract(): jnp.einsum('srkc,kcq->srq', tiles, values, precision=lax.Precision.HIGHES...]
  transfers between devices with their start and end apart: 3 -> 0, of which waited for: 3 -> 0; matrix products, arithmetic and copies ran while one was open for 0% -> 0% of each run, Pallas kernels for 0% -> 0%
where the time goes in v1:
time: 70.2 us; the launch traced here: 70 us
  Pallas kernels  66.5 us (95%)
  local copies, waits for them, and re-layouts  3.49 us (5%)
    pallas_call x1, Pallas kernels, local(): pl.pallas_call(functools.partial(kernel, side, planes), name='falkon', ou...  66.5 us
    unnamed x7, local copies, waits for them, and re-layouts  3.49 us

profile of v1, /device:TPU:1, one launch (start us, length us, event | category | flops | bytes accessed | tf_op | source)
XLA Modules:
  0.0 70.0 jit_solution(8390385897726341139)
XLA Ops:
  0.0 0.0 copy-start
  0.0 1.0 %copy-done = f32[2,512,128]{2,1,0:T(8,128)S(1)} copy-done((f32[2,512,128]{2,1,0:T(8,128)S(1)}, f32[2,512,128]{2,1,0:T(8,128)}, u32[]{:S(2)}) %copy-start) | copy-done | bytes 524312
  1.0 0.0 copy-start.1
  1.0 0.9 %copy-done.1 = f32[18,16,64]{2,1,0:T(8,128)S(1)} copy-done((f32[18,16,64]{2,1,0:T(8,128)S(1)}, f32[18,16,64]{2,1,0:T(8,128)}, u32[]{:S(2)}) %copy-start.1) | copy-done | bytes 73752
  2.0 0.0 copy-start.2
  2.0 0.8 %copy-done.2 = f32[2,128,64]{1,2,0:T(8,128)S(1)} copy-done((f32[2,128,64]{1,2,0:T(8,128)S(1)}, f32[2,128,64]{1,2,0:T(8,128)}, u32[]{:S(2)}) %copy-start.2) | copy-done | bytes 65560
  2.8 66.5 %falkon.1 = f32[2,64,512]{2,1,0:T(8,128)S(1)} custom-call(f32[2,20,128,512]{3,2,1,0:T(8,128)} %bitcast.5, f32[2,512,128]{2,1,0:T(8,128)S(1)} %copy-done, f32[2,64,128]{2,1,0:T(8,128)S(1)} %bitcast.4, f32[18,16,64]{2,1,0:T(8,128)S(1)} %copy-done.1), custom_call_target="tpu_custom_call" | custom-call | tf_op jit(solution)/shard_map/falkon/pallas_call | solution.py:282
  69.3 0.7 %copy.6 = f32[2,512,64]{1,2,0:T(8,128)} copy(f32[2,512,64]{1,2,0:T(8,128)S(1)} %bitcast.3) | data formatting | bytes 524288
Async XLA Ops:
  0.0 1.0 %copy-start = (f32[2,512,128]{2,1,0:T(8,128)S(1)}, f32[2,512,128]{2,1,0:T(8,128)}, u32[]{:S(2)}) copy-start(f32[2,512,128]{2,1,0:T(8,128)} %inverses.1) | copy-start | bytes 1572868
  1.0 0.9 %copy-start.1 = (f32[18,16,64]{2,1,0:T(8,128)S(1)}, f32[18,16,64]{2,1,0:T(8,128)}, u32[]{:S(2)}) copy-start(f32[18,16,64]{2,1,0:T(8,128)} %earlier.1) | copy-start | bytes 221188
  2.0 0.8 %copy-start.2 = (f32[2,128,64]{1,2,0:T(8,128)S(1)}, f32[2,128,64]{1,2,0:T(8,128)}, u32[]{:S(2)}) copy-start(f32[2,128,64]{1,2,0:T(8,128)} %param.6) | copy-start | bytes 196612

commit v2 on v0

v2 whole, which is shorter than its diff:
```python
import functools

import jax
import jax.numpy as jnp
from jax import lax
from jax.experimental import pallas as pl
from jax.experimental.pallas import tpu as pltpu
from jax.sharding import PartitionSpec as P

MESH = pl.DeviceIdType.MESH
F32 = jnp.float32
BF16 = jnp.bfloat16
CORES = 2
HALVES = 2
CHUNKS = (((0, 1, 4), (2, 3)), ((5,), (7,)), ((6,), (8,)))


def split(value):
    high = value.astype(BF16)
    return high, (value - high.astype(F32)).astype(BF16)


def product(left, right):
    return jnp.dot(left, right, preferred_element_type=F32)


def kernel(
    side, planes, factor, inverses, right_side, earlier, solved,
    known_00, known_01, known_10, known_11, known_20, known_21, weights, tiles, tiles_split, corner, inverse, inverse_split, corner_split,
    right, early, mine, others, term, parts, value,
    load_sem, ring_send, group_send, core_send, ring_sem, group_sem, core_sem,
    z_send, z_sem, first_send, first_sem, second_send, second_sem,
):
    known = ((known_00, known_01), (known_10, known_11), (known_20, known_21))
    steps, prior, rows, width = tiles.shape
    outs = right_side.shape[1]
    outs_half = outs // HALVES
    place = lax.axis_index("row")
    z = lax.axis_index("col")
    y, x, core = place // (side * CORES), (place // CORES) % side, place % CORES

    def device(dy, dx, other=0):
        to_core = core + other * (1 - 2 * core)
        return (((y + dy) % side * side + (x + dx) % side) * CORES + to_core, z)

    def above(dz):
        return (place, (z + dz) % planes)

    sibling = (place + 1 - 2 * core, z)
    far_ring = [2, 1, 3]
    near_first = [1, 3, 2]
    greeted = [(d * turn, d * (1 - turn), other) for d in far_ring for turn in (0, 1) for other in (0, 1)]
    z_far_first = sorted(range(1, planes), key=lambda d: -min(d, planes - d))

    barrier = pltpu.get_barrier_semaphore()
    for dz in z_far_first:
        pl.semaphore_signal(barrier, inc=1, device_id=above(dz), device_id_type=MESH)
    for place_of in greeted:
        pl.semaphore_signal(barrier, inc=1, device_id=device(*place_of), device_id_type=MESH)
    pl.semaphore_signal(barrier, inc=1, device_id=sibling, device_id_type=MESH)

    copies = []

    def load(source, target):
        copy = pltpu.make_async_copy(source, target, load_sem.at[len(copies)])
        copy.start()
        copies.append(copy)
        return copy

    load_early = load(earlier, early)
    group = 3
    load_tiles = [[], []]

    def load_step(step):
        for at in range(prior // group):
            blocks = pl.ds(at * group, group)
            load_tiles[step].append(load(factor.at[step, blocks], tiles.at[step, blocks]))

    load_step(0)
    load_right = load(right_side, right)
    load_inverse = load(inverses, inverse)
    load_corner = load(factor.at[1, prior], corner)
    load_step(1)

    turns = [(part + core) % 2 for part in range(2)]
    outer = [y * (1 - turn) + x * turn for turn in turns]
    inner = [x * (1 - turn) + y * turn for turn in turns]
    load_early.wait()
    for chunk, parts_of in enumerate(CHUNKS):
        for part, units in enumerate(parts_of):
            for at, unit in enumerate(units):
                if unit == 4:
                    pieces = [early[16], early[17]]
                else:
                    first = 4 * (unit % 5)
                    columns = slice(0, outs_half) if unit < 4 else slice(outs_half, outs)
                    pieces = [early[first + block, :, columns] for block in range(4)]
                known[chunk][part][core, outer[part], inner[part], at] = jnp.concatenate(pieces, axis=1)

    pl.semaphore_wait(barrier, len(greeted) + planes)

    def ring(part, distance):
        return device(distance * turns[part], distance * (1 - turns[part]))

    def across(part, distance):
        return device(distance * (1 - turns[part]), distance * turns[part])

    def remote(source, target, send, recv, to):
        return pltpu.make_async_remote_copy(
            src_ref=source, dst_ref=target, send_sem=send, recv_sem=recv, device_id=to, device_id_type=MESH
        )

    def piece(chunk, part, distance):
        return known[chunk][part].at[core, outer[part], (inner[part] + distance) % side]

    def whole(chunk, part, distance):
        return known[chunk][part].at[core, (outer[part] + distance) % side]

    def whole_other(chunk, part, distance):
        return known[chunk][part].at[1 - core, (inner[part] + distance) % side]

    def go_round(chunk, part, distance):
        own = piece(chunk, part, 0)
        return remote(own, own, ring_send.at[chunk], ring_sem.at[chunk, part, distance], ring(part, distance))

    def go_across(chunk, part, held, distance):
        own = piece(chunk, part, held)
        return remote(own, own, group_send.at[chunk], group_sem.at[chunk, part, distance], across(part, distance))

    def go_over(chunk, part, distance):
        own = whole(chunk, part, distance)
        return remote(own, own, core_send.at[chunk], core_sem.at[chunk, part, distance], sibling)

    chunks = range(len(CHUNKS))

    def drain():
        for chunk in chunks:
            for part in range(2):
                for sent, got in (
                    (ring_send, known[chunk][part].at[0, 0, pl.ds(0, side - 1)]),
                    (group_send, known[chunk][part].at[0, pl.ds(0, side - 1)]),
                    (core_send, known[chunk][part].at[0]),
                ):
                    remote(got, got, sent.at[chunk], ring_sem.at[0, 0, 0], sibling).wait_send()
        for step in range(steps):
            for half in range(HALVES):
                got = others.at[step, half]
                remote(got, got, z_send.at[step, half], z_sem.at[step, half], sibling).wait_send()
                for way in range(2):
                    got = parts.at[step, half, way, pl.ds(0, CORES * side - 1)]
                    remote(got, got, first_send.at[step, half, way], z_sem.at[step, half], sibling).wait_send()
                    remote(got, got, second_send.at[step, half, way], z_sem.at[step, half], sibling).wait_send()

    for chunk in chunks:
        for distance in far_ring:
            for part in range(2):
                go_round(chunk, part, distance).start()
        for distance in far_ring:
            for part in range(2):
                go_across(chunk, part, 0, distance).start()

    def cut(step, at):
        load_tiles[step][at].wait()

        def one(block, carry):
            high, low = split(tiles[step, block])
            tiles_split[step, block, 0:rows] = high
            tiles_split[step, block, rows : 2 * rows] = low
            return carry

        lax.fori_loop(at * group, (at + 1) * group, one, 0)

    lane = lax.broadcasted_iota(jnp.int32, (rows, 128), 1)

    def unpack(chunk, part, distance, other):
        at_outer = ((inner if other else outer)[part] + distance) % side
        turn = 1 - turns[part] if other else turns[part]
        at_core = 1 - core if other else core
        for at_inner in range(side):
            at_y, at_x = at_outer * (1 - turn) + at_inner * turn, at_inner * (1 - turn) + at_outer * turn
            row = pl.multiple_of(((at_y * side + at_x) * CORES + at_core) * 16, 16)
            for at, unit in enumerate(CHUNKS[chunk][part]):
                high, low = split(known[chunk][part][at_core, at_outer, at_inner, at])
                weights[unit, pl.ds(row, 16), 0:128] = high
                weights[unit, pl.ds(row, 16), 128:256] = low

    def ring_in(chunk):
        for distance in near_first:
            for part in range(2):
                go_round(chunk, part, distance).wait_recv()
                for onward in far_ring:
                    go_across(chunk, part, side - distance, onward).start()
        for part in range(2):
            go_over(chunk, part, 0).start()

    def across_in(chunk):
        for part in range(2):
            unpack(chunk, part, 0, False)
        for distance in near_first:
            for part in range(2):
                got = whole(chunk, part, side - distance)
                remote(got, got, group_send.at[chunk], group_sem.at[chunk, part, distance], sibling).wait_recv()
                go_over(chunk, part, side - distance).start()
                unpack(chunk, part, side - distance, False)

    def over_in(chunk):
        for distance in [0] + near_first:
            for part in range(2):
                got = whole_other(chunk, part, distance)
                remote(got, got, core_send.at[chunk], core_sem.at[chunk, part, distance], sibling).wait_recv()
                unpack(chunk, part, distance, True)

    def multiply(step, units):
        total = None
        for unit in units:
            first = 4 * (unit % 5)
            left = tiles_split[step, first : first + 4].reshape(4 * 2 * rows, width)
            term_of = product(left, weights[unit])
            total = term_of if total is None else total + term_of
        found = None
        for block in reversed(range(4)):
            at = 2 * rows * block
            both = total[at : at + rows] + total[at + rows : at + 2 * rows]
            both = both[:, 0:128] + both[:, 128:256]
            found = both if found is None else jnp.where(lane < outs_half * (block + 1), both, found)
        turned = jnp.transpose(found)
        return (turned[0:32] + turned[32:64]) + (turned[64:96] + turned[96:128])

    def multiply_last(step):
        total = product(tiles_split[step, 16:18].reshape(2 * 2 * rows, width), weights[4])
        found = None
        for block in reversed(range(2)):
            at = 2 * rows * block
            both = total[at : at + rows] + total[at + rows : at + 2 * rows]
            both = both[:, 0:128] + both[:, 128:256]
            found = both if found is None else jnp.where(lane < outs, both, found)
        turned = jnp.transpose(found)
        return turned[0:outs] + turned[outs : 2 * outs]

    def send_up(step, half, part_sum):
        mine[step, half] = part_sum
        for dz in z_far_first:
            remote(
                mine.at[step, half], others.at[step, half, dz - 1], z_send.at[step, half], z_sem.at[step, half], above(dz)
            ).start()

    all_loads = prior // group
    cut(0, 0)
    cut(0, 1)
    ring_in(0)
    cut(0, 2)
    cut(0, 3)
    ring_in(1)
    ring_in(2)
    cut(0, 4)
    cut(0, 5)

    load_inverse.wait()
    for step in range(steps):
        high, low = split(jnp.transpose(inverse[step]))
        inverse_split[step, 0, 0:rows] = high
        inverse_split[step, 0, rows : 2 * rows] = high
        inverse_split[step, 1, 0:rows] = low
        inverse_split[step, 1, rows : 2 * rows] = low
    load_corner.wait()
    high, low = split(jnp.transpose(corner[...]))
    corner_split[:, 0:rows] = high
    corner_split[:, rows : 2 * rows] = low

    across_in(0)
    over_in(0)
    last_two = multiply_last(0)
    send_up(0, 0, multiply(0, (0, 1, 2, 3)) + last_two[0:outs_half])
    across_in(1)
    across_in(2)
    over_in(1)
    partial = multiply(0, (5, 7)) + last_two[outs_half:outs]
    over_in(2)
    send_up(0, 1, partial + multiply(0, (6, 8)))

    coordinates = (x, y)
    groups = range(width // 128)

    def along(way, distance, other):
        return device(distance * way, distance * (1 - way), other)

    def take_planes(step, half):
        got = others.at[step, half]
        remote(got, got, z_send.at[step, half], z_sem.at[step, half], sibling).wait_recv()
        total = mine[step, half]
        for dz in range(planes - 1):
            total = total + others[step, half, dz]
        high, low = split(right[step, half * outs_half : (half + 1) * outs_half] - total)
        both = jnp.concatenate([high, low], axis=1)
        result = product(both, inverse_split[step, 0]) + product(both, inverse_split[step, 1])
        for at in groups:
            term[step, half, at] = result[:, 128 * at : 128 * at + 128]
        for way in range(2):
            slot = CORES * coordinates[way] + core
            parts[step, half, way, slot] = term[step, half, 2 * way + core]
            for distance in far_ring + [0]:
                for other in (0, 1) if distance else (1,):
                    remote(
                        term.at[step, half, 2 * way + core + other * (1 - 2 * core)], parts.at[step, half, way, slot],
                        first_send.at[step, half, way], first_sem.at[step, half, way], along(way, distance, other),
                    ).start()

    def take_first(step, half):
        for way in range(2):
            got = parts.at[step, half, way, pl.ds(0, CORES * side - 1)]
            remote(got, got, first_send.at[step, half, way], first_sem.at[step, half, way], sibling).wait_recv()
            total = parts[step, half, way, 0]
            for slot in range(1, CORES * side):
                total = total + parts[step, half, way, slot]
            slot = coordinates[1 - way]
            value[step, half, 2 * way + core, slot] = total
            own = value.at[step, half, 2 * way + core, slot]
            for distance in far_ring + [0]:
                for other in (0, 1) if distance else (1,):
                    remote(
                        own, own, second_send.at[step, half, way], second_sem.at[step, half, way, other],
                        along(1 - way, distance, other),
                    ).start()

    def take_second(step, half):
        for way in range(2):
            for other in (0, 1):
                got = value.at[step, half, 2 * way, pl.ds(0, side - 1 + other)]
                remote(
                    got, got, second_send.at[step, half, way], second_sem.at[step, half, way, other], sibling
                ).wait_recv()
        last = []
        for at in groups:
            total = value[step, half, at, 0]
            for slot in range(1, side):
                total = total + value[step, half, at, slot]
            last.append(total)
        last = jnp.concatenate(last, axis=1)
        solved[step, half * outs_half : (half + 1) * outs_half] = last
        return last

    load_right.wait()
    for at in range(all_loads):
        cut(1, at)
    later = []
    for step in range(steps):
        take_planes(step, 0)
        if step == 0:
            last_two = multiply_last(1)
            later = [
                multiply(1, range(5 * half, 5 * half + 4)) + last_two[half * outs_half : (half + 1) * outs_half]
                for half in range(HALVES)
            ]
        take_planes(step, 1)
        for half in range(HALVES):
            take_first(step, half)
        for half in range(HALVES):
            last = take_second(step, half)
            if step + 1 < steps:
                high, low = split(last)
                update = product(jnp.concatenate([high, low], axis=0), corner_split[...])
                update = update[:, 0:rows] + update[:, rows : 2 * rows]
                update = update[0:outs_half] + update[outs_half : 2 * outs_half]
                send_up(step + 1, half, later[half] + update)

    drain()


def local(side, planes, factor, inverses, right_side, earlier):
    steps, rows, _, width = factor.shape
    prior, share, outs = earlier.shape
    outs_half = outs // HALVES
    chunks = len(CHUNKS)
    dma, vmem = pltpu.SemaphoreType.DMA, pltpu.VMEM
    in_hbm = pl.BlockSpec(memory_space=pltpu.HBM)
    solved = pl.pallas_call(
        functools.partial(kernel, side, planes),
        name="falkon",
        out_shape=jax.ShapeDtypeStruct((steps, outs, width), F32),
        in_specs=[in_hbm] * 4,
        out_specs=pl.BlockSpec(memory_space=pltpu.VMEM),
        scratch_shapes=[
            *[vmem((CORES, side, side, len(units), 16, 128), F32) for chunk in CHUNKS for units in chunk],
            vmem((9, width, 256), BF16),
            vmem((steps, prior, rows, width), F32),
            vmem((steps, prior, 2 * rows, width), BF16),
            vmem((rows, width), F32),
            vmem((steps, width, rows), F32),
            vmem((steps, 2, 2 * rows, width), BF16),
            vmem((width, 2 * rows), BF16),
            vmem((steps, outs, rows), F32),
            vmem((prior, share, outs), F32),
            vmem((steps, HALVES, outs_half, rows), F32),
            vmem((steps, HALVES, planes - 1, outs_half, rows), F32),
            vmem((steps, HALVES, 2 * CORES, outs_half, 128), F32),
            vmem((steps, HALVES, 2, CORES * side, outs_half, 128), F32),
            vmem((steps, HALVES, 2 * CORES, side, outs_half, 128), F32),
            dma((16,)),
            dma((chunks,)),
            dma((chunks,)),
            dma((chunks,)),
            dma((chunks, 2, side)),
            dma((chunks, 2, side)),
            dma((chunks, 2, side)),
            dma((steps, HALVES)),
            dma((steps, HALVES)),
            dma((steps, HALVES, 2)),
            dma((steps, HALVES, 2)),
            dma((steps, HALVES, 2)),
            dma((steps, HALVES, 2, 2)),
        ],
        compiler_params=pltpu.CompilerParams(
            collective_id=0, has_side_effects=True, vmem_limit_bytes=40 << 20
        ),
    )(
        *[
            pltpu.with_memory_space_constraint(array, pltpu.HBM)
            for array in (
                jnp.transpose(factor, (0, 2, 1, 3)),
                inverses,
                jnp.transpose(right_side, (0, 2, 1)),
                earlier,
            )
        ]
    )
    return jnp.transpose(solved, (0, 2, 1))


def solution(mesh):
    side = 1
    while side * side * CORES < mesh.shape["row"]:
        side += 1
    in_specs = (
        P(None, "row", None, "col"),
        P(None, "col", "row"),
        P(None, "row", None),
        P(None, ("col", "row"), None),
    )
    return jax.shard_map(
        functools.partial(local, side, mesh.shape["col"]),
        mesh=mesh,
        in_specs=in_specs,
        out_specs=P(None, "col", None),
        check_vma=False,
    )
```

time: 366 us -> 56.7 us (0.15)
  waiting for transfers between devices: 291 us -> 0 us
  Pallas kernels: 0 us -> 55.9 us
  blocking collectives: 46.1 us -> 0 us
  matrix products: 14.6 us -> 0 us
  between operations: 13.1 us -> 0.01 us
    psum x2 -> x0, waiting for transfers between devices: 228 us -> none  [local(): value = lax.psum(term, 'row')]
    all_gather x1 -> x0, waiting for transfers between devices: 62.3 us -> none  [local(): lax.all_gather(earlier, 'row', axis=1, tiled=True)]
    pallas_call x0 -> x1, Pallas kernels: none -> 55.9 us  [local(): pl.pallas_call(functools.partial(kernel, side, planes), name='falkon', ou...]
    psum x2 -> x0, blocking collectives: 46.1 us -> none  [column_total(): return lax.psum(partial_value, 'col')]
    dot_general x4 -> x0, matrix products: 14.6 us -> none  [the longest x1 11 us: contract(): jnp.einsum('srkc,kcq->srq', tiles, values, precision=lax.Precision.HIGHES...]
  transfers between devices with their start and end apart: 3 -> 0, of which waited for: 3 -> 0; matrix products, arithmetic and copies ran while one was open for 0% -> 0% of each run, Pallas kernels for 0% -> 0%
where the time goes in v2:
time: 56.7 us; the launch traced here: 56.6 us
  Pallas kernels  55.9 us (99%)
  local copies, waits for them, and re-layouts  0.71 us (1%)
    pallas_call x1, Pallas kernels, local(): pl.pallas_call(functools.partial(kernel, side, planes), name='falkon', ou...  55.9 us

profile of v2, /device:TPU:1, one launch (start us, length us, event | category | flops | bytes accessed | tf_op | source)
XLA Modules:
  0.0 56.6 jit_solution(17046337682603326912)
XLA Ops:
  0.0 55.9 %falkon.1 = f32[2,64,512]{2,1,0:T(8,128)S(1)} custom-call(f32[2,20,128,512]{3,2,1,0:T(8,128)} %bitcast.4, f32[2,512,128]{2,1,0:T(8,128)} %inverses.1, f32[2,64,128]{2,1,0:T(8,128)} %bitcast.5, f32[18,16,64]{2,1,0:T(8,128)} %earlier.1), custom_call_target="tpu_custom_call" | custom-call | tf_op jit(solution)/shard_map/falkon/pallas_call | solution.py:376
  55.9 0.7 %copy.6 = f32[2,512,64]{1,2,0:T(8,128)} copy(f32[2,512,64]{1,2,0:T(8,128)S(1)} %bitcast.3) | data formatting | bytes 524288

commit v3 on v2

--- a/solution.py
+++ b/solution.py
@@ -29,7 +29,7 @@
     known_00, known_01, known_10, known_11, known_20, known_21, weights, tiles, tiles_split, corner, inverse, inverse_split, corner_split,
     right, early, mine, others, term, parts, value,
     load_sem, ring_send, group_send, core_send, ring_sem, group_sem, core_sem,
-    z_send, z_sem, first_send, first_sem, second_send, second_sem,
+    z_send, z_sem, first_send, first_sem, second_send, second_sem, vouch_sem,
 ):
     known = ((known_00, known_01), (known_10, known_11), (known_20, known_21))
     steps, prior, rows, width = tiles.shape
@@ -49,15 +49,13 @@
     sibling = (place + 1 - 2 * core, z)
     far_ring = [2, 1, 3]
     near_first = [1, 3, 2]
-    greeted = [(d * turn, d * (1 - turn), other) for d in far_ring for turn in (0, 1) for other in (0, 1)]
     z_far_first = sorted(range(1, planes), key=lambda d: -min(d, planes - d))
 
+    greeted = [device(d * turn, d * (1 - turn)) for d in far_ring for turn in (0, 1)]
+    greeted += [above(dz) for dz in (2, planes - 2, 1, planes - 1)] + [sibling]
     barrier = pltpu.get_barrier_semaphore()
-    for dz in z_far_first:
-        pl.semaphore_signal(barrier, inc=1, device_id=above(dz), device_id_type=MESH)
-    for place_of in greeted:
-        pl.semaphore_signal(barrier, inc=1, device_id=device(*place_of), device_id_type=MESH)
-    pl.semaphore_signal(barrier, inc=1, device_id=sibling, device_id_type=MESH)
+    for to in greeted:
+        pl.semaphore_signal(barrier, inc=1, device_id=to, device_id_type=MESH)
 
     copies = []
 
@@ -97,7 +95,10 @@
                     pieces = [early[first + block, :, columns] for block in range(4)]
                 known[chunk][part][core, outer[part], inner[part], at] = jnp.concatenate(pieces, axis=1)
 
-    pl.semaphore_wait(barrier, len(greeted) + planes)
+    pl.semaphore_wait(barrier, len(greeted))
+    vouched_by = [above(2), above(planes - 2), sibling]
+    for to in vouched_by:
+        pl.semaphore_signal(vouch_sem, inc=1, device_id=to, device_id_type=MESH)
 
     def ring(part, distance):
         return device(distance * turns[part], distance * (1 - turns[part]))
@@ -151,10 +152,12 @@
                     remote(got, got, first_send.at[step, half, way], z_sem.at[step, half], sibling).wait_send()
                     remote(got, got, second_send.at[step, half, way], z_sem.at[step, half], sibling).wait_send()
 
-    for chunk in chunks:
+    def ring_out(chunk):
         for distance in far_ring:
             for part in range(2):
                 go_round(chunk, part, distance).start()
+
+    def across_out(chunk):
         for distance in far_ring:
             for part in range(2):
                 go_across(chunk, part, 0, distance).start()
@@ -193,15 +196,14 @@
         for part in range(2):
             go_over(chunk, part, 0).start()
 
-    def across_in(chunk):
-        for part in range(2):
-            unpack(chunk, part, 0, False)
-        for distance in near_first:
-            for part in range(2):
-                got = whole(chunk, part, side - distance)
-                remote(got, got, group_send.at[chunk], group_sem.at[chunk, part, distance], sibling).wait_recv()
-                go_over(chunk, part, side - distance).start()
-                unpack(chunk, part, side - distance, False)
+    def across_in(chunk, distances=(0, *near_first)):
+        for distance in distances:
+            for part in range(2):
+                if distance > 0:
+                    got = whole(chunk, part, side - distance)
+                    remote(got, got, group_send.at[chunk], group_sem.at[chunk, part, distance], sibling).wait_recv()
+                    go_over(chunk, part, side - distance).start()
+                unpack(chunk, part, (side - distance) % side, False)
 
     def over_in(chunk):
         for distance in [0] + near_first:
@@ -244,31 +246,40 @@
                 mine.at[step, half], others.at[step, half, dz - 1], z_send.at[step, half], z_sem.at[step, half], above(dz)
             ).start()
 
+    def prepare():
+        load_inverse.wait()
+        for step in range(steps):
+            high, low = split(jnp.transpose(inverse[step]))
+            inverse_split[step, 0, 0:rows] = high
+            inverse_split[step, 0, rows : 2 * rows] = high
+            inverse_split[step, 1, 0:rows] = low
+            inverse_split[step, 1, rows : 2 * rows] = low
+        load_corner.wait()
+        high, low = split(jnp.transpose(corner[...]))
+        corner_split[:, 0:rows] = high
+        corner_split[:, rows : 2 * rows] = low
+
     all_loads = prior // group
+    ring_out(0)
+    across_out(0)
+    ring_out(1)
+    ring_out(2)
     cut(0, 0)
     cut(0, 1)
     ring_in(0)
+    across_out(1)
     cut(0, 2)
     cut(0, 3)
-    ring_in(1)
-    ring_in(2)
     cut(0, 4)
     cut(0, 5)
-
-    load_inverse.wait()
-    for step in range(steps):
-        high, low = split(jnp.transpose(inverse[step]))
-        inverse_split[step, 0, 0:rows] = high
-        inverse_split[step, 0, rows : 2 * rows] = high
-        inverse_split[step, 1, 0:rows] = low
-        inverse_split[step, 1, rows : 2 * rows] = low
-    load_corner.wait()
-    high, low = split(jnp.transpose(corner[...]))
-    corner_split[:, 0:rows] = high
-    corner_split[:, rows : 2 * rows] = low
-
-    across_in(0)
+    prepare()
+    ring_in(1)
+    across_in(0, (0, 1))
+    across_out(2)
+    ring_in(2)
+    across_in(0, (3, 2))
     over_in(0)
+    pl.semaphore_wait(vouch_sem, len(vouched_by))
     last_two = multiply_last(0)
     send_up(0, 0, multiply(0, (0, 1, 2, 3)) + last_two[0:outs_half])
     across_in(1)
@@ -408,6 +419,7 @@
             dma((steps, HALVES, 2)),
             dma((steps, HALVES, 2)),
             dma((steps, HALVES, 2, 2)),
+            pltpu.SemaphoreType.REGULAR,
         ],
         compiler_params=pltpu.CompilerParams(
             collective_id=0, has_side_effects=True, vmem_limit_bytes=40 << 20

time: 56.7 us -> 55.6 us (0.981)
  Pallas kernels: 55.9 us -> 54.8 us
    pallas_call x1, Pallas kernels: 55.9 us -> 54.8 us  [local(): pl.pallas_call(functools.partial(kernel, side, planes), name='falkon', ou...]
where the time goes in v3:
time: 55.6 us; the launch traced here: 55.5 us
  Pallas kernels  54.8 us (99%)
  local copies, waits for them, and re-layouts  0.71 us (1%)
    pallas_call x1, Pallas kernels, local(): pl.pallas_call(functools.partial(kernel, side, planes), name='falkon', ou...  54.8 us

profile of v3, /device:TPU:1, one launch (start us, length us, event | category | flops | bytes accessed | tf_op | source)
XLA Modules:
  0.0 55.5 jit_solution(8666543204920378846)
XLA Ops:
  0.0 54.8 %falkon.1 = f32[2,64,512]{2,1,0:T(8,128)S(1)} custom-call(f32[2,20,128,512]{3,2,1,0:T(8,128)} %bitcast.4, f32[2,512,128]{2,1,0:T(8,128)} %inverses.1, f32[2,64,128]{2,1,0:T(8,128)} %bitcast.5, f32[18,16,64]{2,1,0:T(8,128)} %earlier.1), custom_call_target="tpu_custom_call" | custom-call | tf_op jit(solution)/shard_map/falkon/pallas_call | solution.py:387
  54.8 0.7 %copy.6 = f32[2,512,64]{1,2,0:T(8,128)} copy(f32[2,512,64]{1,2,0:T(8,128)S(1)} %bitcast.3) | data formatting | bytes 524288

commit v4 on v3

--- a/solution.py
+++ b/solution.py
@@ -290,6 +290,7 @@
     send_up(0, 1, partial + multiply(0, (6, 8)))
 
     coordinates = (x, y)
+    in_plane = ((2, 1), (2, 0), (1, 1), (3, 1), (1, 0), (3, 0), (0, 1))
     groups = range(width // 128)
 
     def along(way, distance, other):
@@ -309,12 +310,11 @@
         for way in range(2):
             slot = CORES * coordinates[way] + core
             parts[step, half, way, slot] = term[step, half, 2 * way + core]
-            for distance in far_ring + [0]:
-                for other in (0, 1) if distance else (1,):
-                    remote(
-                        term.at[step, half, 2 * way + core + other * (1 - 2 * core)], parts.at[step, half, way, slot],
-                        first_send.at[step, half, way], first_sem.at[step, half, way], along(way, distance, other),
-                    ).start()
+            for distance, other in in_plane:
+                remote(
+                    term.at[step, half, 2 * way + core + other * (1 - 2 * core)], parts.at[step, half, way, slot],
+                    first_send.at[step, half, way], first_sem.at[step, half, way], along(way, distance, other),
+                ).start()
 
     def take_first(step, half):
         for way in range(2):
@@ -326,12 +326,11 @@
             slot = coordinates[1 - way]
             value[step, half, 2 * way + core, slot] = total
             own = value.at[step, half, 2 * way + core, slot]
-            for distance in far_ring + [0]:
-                for other in (0, 1) if distance else (1,):
-                    remote(
-                        own, own, second_send.at[step, half, way], second_sem.at[step, half, way, other],
-                        along(1 - way, distance, other),
-                    ).start()
+            for distance, other in in_plane:
+                remote(
+                    own, own, second_send.at[step, half, way], second_sem.at[step, half, way, other],
+                    along(1 - way, distance, other),
+                ).start()
 
     def take_second(step, half):
         for way in range(2):

time: 55.6 us -> 55 us (0.989)
  Pallas kernels: 54.8 us -> 54.2 us
where the time goes in v4:
time: 55 us
  Pallas kernels  54.2 us (99%)
  local copies, waits for them, and re-layouts  0.71 us (1%)
    pallas_call x1, Pallas kernels, local(): pl.pallas_call(functools.partial(kernel, side, planes), name='falkon', ou...  54.2 us

profile of v4, /device:TPU:1, one launch (start us, length us, event | category | flops | bytes accessed | tf_op | source)
XLA Modules:
  0.0 55.0 jit_solution(10431165523802001838)
XLA Ops:
  0.0 54.2 %falkon.1 = f32[2,64,512]{2,1,0:T(8,128)S(1)} custom-call(f32[2,20,128,512]{3,2,1,0:T(8,128)} %bitcast.4, f32[2,512,128]{2,1,0:T(8,128)} %inverses.1, f32[2,64,128]{2,1,0:T(8,128)} %bitcast.5, f32[18,16,64]{2,1,0:T(8,128)} %earlier.1), custom_call_target="tpu_custom_call" | custom-call | tf_op jit(solution)/shard_map/falkon/pallas_call | solution.py:386
  54.3 0.7 %copy.6 = f32[2,512,64]{1,2,0:T(8,128)} copy(f32[2,512,64]{1,2,0:T(8,128)S(1)} %bitcast.3) | data formatting | bytes 524288

commit v5 on v4

--- a/solution.py
+++ b/solution.py
@@ -51,21 +51,22 @@
     near_first = [1, 3, 2]
     z_far_first = sorted(range(1, planes), key=lambda d: -min(d, planes - d))
 
+    copies = []
+
+    def load(source, target):
+        copy = pltpu.make_async_copy(source, target, load_sem.at[len(copies)])
+        copy.start()
+        copies.append(copy)
+        return copy
+
+    load_early = load(earlier, early)
+
     greeted = [device(d * turn, d * (1 - turn)) for d in far_ring for turn in (0, 1)]
     greeted += [above(dz) for dz in (2, planes - 2, 1, planes - 1)] + [sibling]
     barrier = pltpu.get_barrier_semaphore()
     for to in greeted:
         pl.semaphore_signal(barrier, inc=1, device_id=to, device_id_type=MESH)
 
-    copies = []
-
-    def load(source, target):
-        copy = pltpu.make_async_copy(source, target, load_sem.at[len(copies)])
-        copy.start()
-        copies.append(copy)
-        return copy
-
-    load_early = load(earlier, early)
     group = 3
     load_tiles = [[], []]
 
@@ -84,8 +85,8 @@
     outer = [y * (1 - turn) + x * turn for turn in turns]
     inner = [x * (1 - turn) + y * turn for turn in turns]
     load_early.wait()
-    for chunk, parts_of in enumerate(CHUNKS):
-        for part, units in enumerate(parts_of):
+    def pack(chunk):
+        for part, units in enumerate(CHUNKS[chunk]):
             for at, unit in enumerate(units):
                 if unit == 4:
                     pieces = [early[16], early[17]]
@@ -95,6 +96,7 @@
                     pieces = [early[first + block, :, columns] for block in range(4)]
                 known[chunk][part][core, outer[part], inner[part], at] = jnp.concatenate(pieces, axis=1)
 
+    pack(0)
     pl.semaphore_wait(barrier, len(greeted))
     vouched_by = [above(2), above(planes - 2), sibling]
     for to in vouched_by:
@@ -262,6 +264,8 @@
     all_loads = prior // group
     ring_out(0)
     across_out(0)
+    for chunk in chunks[1:]:
+        pack(chunk)
     ring_out(1)
     ring_out(2)
     cut(0, 0)

time: 55 us -> 55 us (level)
  no operation moved by 1% of the time
where the time goes in v5:
time: 55 us
  Pallas kernels  54.2 us (99%)
  local copies, waits for them, and re-layouts  0.71 us (1%)
    pallas_call x1, Pallas kernels, local(): pl.pallas_call(functools.partial(kernel, side, planes), name='falkon', ou...  54.2 us

profile of v5, /device:TPU:1, one launch (start us, length us, event | category | flops | bytes accessed | tf_op | source)
XLA Modules:
  0.0 55.0 jit_solution(9078190456520074634)
XLA Ops:
  0.0 54.2 %falkon.1 = f32[2,64,512]{2,1,0:T(8,128)S(1)} custom-call(f32[2,20,128,512]{3,2,1,0:T(8,128)} %bitcast.4, f32[2,512,128]{2,1,0:T(8,128)} %inverses.1, f32[2,64,128]{2,1,0:T(8,128)} %bitcast.5, f32[18,16,64]{2,1,0:T(8,128)} %earlier.1), custom_call_target="tpu_custom_call" | custom-call | tf_op jit(solution)/shard_map/falkon/pallas_call | solution.py:390
  54.3 0.7 %copy.6 = f32[2,512,64]{1,2,0:T(8,128)} copy(f32[2,512,64]{1,2,0:T(8,128)S(1)} %bitcast.3) | data formatting | bytes 524288
